TPU v7x, 128 devices: a whole 4x4x4 slice. The times are simulated.
128 devices in a mesh: dp: 4 (over x_hi, core), blk: 4 (over z), tensor: 8 (over y, x_lo).
Axes of the slice: x: 4 (x_hi: 2, x_lo: 2; x = x_hi * 2 + x_lo), y: 4, z: 4, core: 2. Of those that a mesh axis runs over, the one named last changes fastest.
Arguments:
- hidden_in: bfloat16 [2048, 12, 1024], P(('blk', 'tensor'), 'dp'), may hold values from -6 to 6
- out_grad: bfloat16 [2048, 12, 1024], P(('blk', 'tensor'), 'dp'), may hold values from -6 to 6
- norm_scales: float32 [2, 1024], replicated, may hold values from 0.1 to 1.9
- norm_shifts: float32 [2, 1024], replicated, may hold values from -3 to 3
- w_qkv: bfloat16 [3, 1024, 1024], P(None, None, 'tensor'), may hold values from -0.25 to 0.25
- w_out: bfloat16 [1024, 1024], P('tensor'), may hold values from -0.75 to 0.75
- w_gate_up: bfloat16 [2, 1024, 4096], P(None, None, 'tensor'), may hold values from -0.1875 to 0.1875
- w_down: bfloat16 [4096, 1024], P('tensor'), may hold values from -0.125 to 0.125
- lengths: int32 [12], P('dp'), may hold values from 256 to 2048, as said below
Outputs:
- result: bfloat16 [2048, 12, 1024], P(('blk', 'tensor'), 'dp')
- grad_input: bfloat16 [2048, 12, 1024], P(('blk', 'tensor'), 'dp')
- grad_qkv: float32 [3, 1024, 1024], P(None, None, 'tensor')
- grad_out_proj: float32 [1024, 1024], P('tensor')
- grad_gate_up: float32 [2, 1024, 4096], P(None, None, 'tensor')
- grad_down: float32 [4096, 1024], P('tensor')
- grad_scales: float32 [2, 1024], replicated
- grad_shifts: float32 [2, 1024], replicated
Inputs may be any that keep to these rules, and one draw needn't show every extreme that they name: `lengths`: each group of 3 consecutive windows (one index of dp) holds at least one window of length 2048; tokens at or past a window's length are padding, whose keys are masked.
All inputs are finite; a program needn't handle non-finite values.
Results may differ from a plain program's by a relative error of at most 0.03.
Values may be sent and summed in bfloat16 or wider, within the bound.
No kernel may reach another device: no remote copies, remote signals or barrier semaphores. Data moves between devices by JAX's collectives and lax.ppermute only.
A program may use at most 192 MiB of HBM per device.

v0:
```python
import jax
import jax.numpy as jnp
from jax import lax
from jax.sharding import PartitionSpec as P

HD = 64


EPSILON = 1e-05
MASKED = -1000000000.0


def norm_rows(values, gain_row, offset_row):
    row_mean = jnp.mean(values, axis=-1, keepdims=True)
    centred = values - row_mean
    row_var = jnp.mean(centred * centred, axis=-1, keepdims=True)
    return centred * lax.rsqrt(row_var + EPSILON) * gain_row + offset_row


def norm_back(values, gain_row, offset_row, cotangent):
    _, pullback = jax.vjp(norm_rows, values, gain_row, offset_row)
    grad_values, grad_gain, grad_offset = pullback(cotangent)
    return (grad_values, grad_gain, grad_offset)


def rope_tables(first_row, length):
    positions = (first_row + jnp.arange(length, dtype=jnp.int32)).astype(jnp.float32)
    inverse = 10000.0 ** (-(jnp.arange(HD // 2, dtype=jnp.float32) * 2.0) / HD)
    angles = positions[:, None] * inverse[None, :]
    angles = jnp.concatenate([angles, angles], axis=-1)
    return (jnp.cos(angles)[:, None, None, :], jnp.sin(angles)[:, None, None, :])


def turn_half(values):
    half_width = values.shape[-1] // 2
    return jnp.concatenate([-values[..., half_width:], values[..., :half_width]], axis=-1)


def rotate_fwd(values, cosine, sine_table):
    return values * cosine + turn_half(values) * sine_table


def rotate_back(values, cosine, sine_table):
    return values * cosine - turn_half(values * sine_table)


def split_heads(values):
    return values.reshape(values.shape[0], values.shape[1], -1, HD)


def key_scores(queries, key_heads, first_row, lengths):
    scores = (
        jnp.einsum("swhc,twhc->whst", queries, key_heads, preferred_element_type=jnp.float32)
        * 0.125
    )
    places = first_row + jnp.arange(key_heads.shape[0], dtype=jnp.int32)
    visible = places[None, :] < lengths[:, None]
    return jnp.where(visible[:, None, None, :], scores, MASKED)


def fold_stats(running, key_piece, first_row, queries, lengths):
    row_top, row_total = running
    scores = key_scores(queries, split_heads(key_piece), first_row, lengths)
    new_top = jnp.maximum(row_top, jnp.max(scores, axis=-1))
    row_total = row_total * jnp.exp(row_top - new_top) + jnp.sum(
        jnp.exp(scores - new_top[..., None]), axis=-1
    )
    return (new_top, row_total)


def fold_values(attended, key_piece, value_piece, first_row, queries, lengths, log_total):
    scores = key_scores(queries, split_heads(key_piece), first_row, lengths)
    weights = jnp.exp(scores - log_total[..., None]).astype(jnp.bfloat16)
    return attended + jnp.einsum(
        "whst,twhc->swhc", weights, split_heads(value_piece), preferred_element_type=jnp.float32
    )


def fold_back(running, pieces, first_row, queries, lengths, log_total, grad_attended, row_delta):
    grad_queries, grad_keys_all, grad_values_all = running
    key_piece, value_piece = pieces
    key_heads = split_heads(key_piece)
    value_heads = split_heads(value_piece)
    scores = key_scores(queries, key_heads, first_row, lengths)
    probabilities = jnp.exp(scores - log_total[..., None])
    grad_weights = jnp.einsum(
        "swhc,twhc->whst", grad_attended, value_heads, preferred_element_type=jnp.float32
    )
    grad_scores = (probabilities * (grad_weights - row_delta[..., None])).astype(jnp.bfloat16)
    grad_queries = grad_queries + 0.125 * jnp.einsum(
        "whst,twhc->swhc", grad_scores, key_heads, preferred_element_type=jnp.float32
    )
    key_term = 0.125 * jnp.einsum(
        "whst,swhc->twhc", grad_scores, queries, preferred_element_type=jnp.float32
    )
    value_term = jnp.einsum(
        "whst,swhc->twhc",
        probabilities.astype(jnp.bfloat16),
        grad_attended,
        preferred_element_type=jnp.float32,
    )
    piece_rows = key_piece.shape[0]
    key_term = key_term.reshape(piece_rows, key_piece.shape[1], -1)
    value_term = value_term.reshape(piece_rows, value_piece.shape[1], -1)
    grad_keys_all = lax.dynamic_update_slice_in_dim(grad_keys_all, key_term, first_row, 0)
    grad_values_all = lax.dynamic_update_slice_in_dim(grad_values_all, value_term, first_row, 0)
    return (grad_queries, grad_keys_all, grad_values_all)


def shards(hidden_in, out_grad, norm_scales, norm_shifts, w_qkv, w_out, w_gate_up, w_down, lengths):
    tensor_count = lax.axis_size("tensor")
    cycle_count = lax.axis_size("blk")
    local_rows = hidden_in.shape[0]
    windows = hidden_in.shape[1]
    block_rows = local_rows * tensor_count
    window_rows = block_rows * cycle_count
    local_width = w_qkv.shape[2]
    inputs = hidden_in.astype(jnp.float32)
    normed_one = norm_rows(inputs, norm_scales[0], norm_shifts[0]).astype(jnp.bfloat16)
    rows_one = lax.all_gather(normed_one, "tensor", axis=0, tiled=True)
    cosine, sine_table = rope_tables(lax.axis_index("blk") * block_rows, block_rows)
    projected = jnp.einsum("swd,kde->kswe", rows_one, w_qkv, preferred_element_type=jnp.float32)
    queries = rotate_fwd(split_heads(projected[0]), cosine, sine_table).astype(jnp.bfloat16)
    keys_own = (
        rotate_fwd(split_heads(projected[1]), cosine, sine_table)
        .astype(jnp.bfloat16)
        .reshape(block_rows, windows, local_width)
    )
    values_own = projected[2].astype(jnp.bfloat16)
    heads_here = queries.shape[2]
    stat_shape = (windows, heads_here, block_rows)
    keys_all, values_all = (
        lax.all_gather(keys_own, "blk", axis=0, tiled=True),
        lax.all_gather(values_own, "blk", axis=0, tiled=True),
    )
    row_top = jnp.full(stat_shape, -1e30, jnp.float32)
    row_total = jnp.zeros(stat_shape, jnp.float32)
    for cycle_step in range(cycle_count):
        first_row = cycle_step * block_rows
        key_piece = lax.slice_in_dim(keys_all, first_row, first_row + block_rows, axis=0)
        row_top, row_total = fold_stats(
            (row_top, row_total), key_piece, first_row, queries, lengths
        )
    log_total = row_top + jnp.log(row_total)
    attended = jnp.zeros((block_rows, windows, heads_here, HD), jnp.float32)
    for cycle_step in range(cycle_count):
        first_row = cycle_step * block_rows
        key_piece = lax.slice_in_dim(keys_all, first_row, first_row + block_rows, axis=0)
        value_piece = lax.slice_in_dim(values_all, first_row, first_row + block_rows, axis=0)
        attended = fold_values(
            attended, key_piece, value_piece, first_row, queries, lengths, log_total
        )
    attended_low = attended.reshape(block_rows, windows, local_width).astype(jnp.bfloat16)
    grad_rows = None
    picked = attended_low
    attn_output = lax.psum_scatter(
        jnp.einsum("swe,ed->swd", picked, w_out, preferred_element_type=jnp.float32).astype(
            jnp.bfloat16
        ),
        "tensor",
        scatter_dimension=0,
        tiled=True,
    ).astype(jnp.float32)
    middle = inputs + attn_output
    normed_two = norm_rows(middle, norm_scales[1], norm_shifts[1]).astype(jnp.bfloat16)
    rows_two = lax.all_gather(normed_two, "tensor", axis=0, tiled=True)
    gate_up = jnp.einsum("swd,kdf->kswf", rows_two, w_gate_up, preferred_element_type=jnp.float32)
    gating = gate_up[0]
    lifted = gate_up[1]
    sigmoid_gate = jax.nn.sigmoid(gating)
    activated = gating * sigmoid_gate
    hidden_low = (activated * lifted).astype(jnp.bfloat16)
    picked = hidden_low
    ffn_output = lax.psum_scatter(
        jnp.einsum("swf,fd->swd", picked, w_down, preferred_element_type=jnp.float32).astype(
            jnp.bfloat16
        ),
        "tensor",
        scatter_dimension=0,
        tiled=True,
    ).astype(jnp.float32)
    result = (middle + ffn_output).astype(jnp.bfloat16)
    grad_rows = lax.all_gather(out_grad, "tensor", axis=0, tiled=True)
    grad_down = jnp.einsum("swf,swd->fd", hidden_low, grad_rows, preferred_element_type=jnp.float32)
    grad_hidden = jnp.einsum("swd,fd->swf", grad_rows, w_down, preferred_element_type=jnp.float32)
    gate_slope = sigmoid_gate * (1.0 + gating * (1.0 - sigmoid_gate))
    grad_gating = (grad_hidden * lifted * gate_slope).astype(jnp.bfloat16)
    grad_lifted = (grad_hidden * activated).astype(jnp.bfloat16)
    grad_gate_up = jnp.stack(
        [
            jnp.einsum("swd,swf->df", rows_two, grad_gating, preferred_element_type=jnp.float32),
            jnp.einsum("swd,swf->df", rows_two, grad_lifted, preferred_element_type=jnp.float32),
        ]
    )
    grad_normed_two = lax.psum_scatter(
        (
            jnp.einsum("swf,df->swd", grad_gating, w_gate_up[0], preferred_element_type=jnp.float32)
            + jnp.einsum(
                "swf,df->swd", grad_lifted, w_gate_up[1], preferred_element_type=jnp.float32
            )
        ).astype(jnp.bfloat16),
        "tensor",
        scatter_dimension=0,
        tiled=True,
    ).astype(jnp.float32)
    grad_middle_norm, grad_scale_two, grad_shift_two = norm_back(
        middle, norm_scales[1], norm_shifts[1], grad_normed_two
    )
    grad_middle = out_grad.astype(jnp.float32) + grad_middle_norm
    grad_attn_rows = lax.all_gather(grad_middle.astype(jnp.bfloat16), "tensor", axis=0, tiled=True)
    grad_out_proj = jnp.einsum(
        "swe,swd->ed", attended_low, grad_attn_rows, preferred_element_type=jnp.float32
    )
    grad_attended = split_heads(
        jnp.einsum("swd,ed->swe", grad_attn_rows, w_out, preferred_element_type=jnp.float32).astype(
            jnp.bfloat16
        )
    )
    row_delta = jnp.sum(grad_attended.astype(jnp.float32) * attended, axis=-1).transpose(1, 2, 0)
    start_state = (
        jnp.zeros((block_rows, windows, heads_here, HD), jnp.float32),
        jnp.zeros((window_rows, windows, local_width), jnp.float32),
        jnp.zeros((window_rows, windows, local_width), jnp.float32),
    )
    back_state = start_state
    for cycle_step in range(cycle_count):
        first_row = cycle_step * block_rows
        key_piece = lax.slice_in_dim(keys_all, first_row, first_row + block_rows, axis=0)
        value_piece = lax.slice_in_dim(values_all, first_row, first_row + block_rows, axis=0)
        back_state = fold_back(
            back_state,
            (key_piece, value_piece),
            first_row,
            queries,
            lengths,
            log_total,
            grad_attended,
            row_delta,
        )
    grad_queries, grad_keys_all, grad_values_all = back_state
    grad_keys_own, grad_values_own = (
        lax.psum_scatter(
            grad_keys_all.astype(jnp.bfloat16), "blk", scatter_dimension=0, tiled=True
        ).astype(jnp.float32),
        lax.psum_scatter(
            grad_values_all.astype(jnp.bfloat16), "blk", scatter_dimension=0, tiled=True
        ).astype(jnp.float32),
    )
    grad_query_pre = (
        rotate_back(grad_queries, cosine, sine_table)
        .reshape(block_rows, windows, local_width)
        .astype(jnp.bfloat16)
    )
    grad_key_pre = (
        rotate_back(split_heads(grad_keys_own), cosine, sine_table)
        .reshape(block_rows, windows, local_width)
        .astype(jnp.bfloat16)
    )
    grad_value_pre = grad_values_own.astype(jnp.bfloat16)
    grad_qkv = jnp.stack(
        [
            jnp.einsum("swd,swe->de", rows_one, grad_query_pre, preferred_element_type=jnp.float32),
            jnp.einsum("swd,swe->de", rows_one, grad_key_pre, preferred_element_type=jnp.float32),
            jnp.einsum("swd,swe->de", rows_one, grad_value_pre, preferred_element_type=jnp.float32),
        ]
    )
    grad_normed_one = lax.psum_scatter(
        (
            jnp.einsum("swe,de->swd", grad_query_pre, w_qkv[0], preferred_element_type=jnp.float32)
            + jnp.einsum("swe,de->swd", grad_key_pre, w_qkv[1], preferred_element_type=jnp.float32)
            + jnp.einsum(
                "swe,de->swd", grad_value_pre, w_qkv[2], preferred_element_type=jnp.float32
            )
        ).astype(jnp.bfloat16),
        "tensor",
        scatter_dimension=0,
        tiled=True,
    ).astype(jnp.float32)
    grad_input_norm, grad_scale_one, grad_shift_one = norm_back(
        inputs, norm_scales[0], norm_shifts[0], grad_normed_one
    )
    grad_input = (grad_middle + grad_input_norm).astype(jnp.bfloat16)
    weight_sums = (
        lax.psum(grad_qkv.astype(jnp.bfloat16), ("dp", "blk")).astype(jnp.float32),
        lax.psum(grad_out_proj.astype(jnp.bfloat16), ("dp", "blk")).astype(jnp.float32),
        lax.psum(grad_gate_up.astype(jnp.bfloat16), ("dp", "blk")).astype(jnp.float32),
        lax.psum(grad_down.astype(jnp.bfloat16), ("dp", "blk")).astype(jnp.float32),
    )
    norm_sums = lax.psum(
        (jnp.stack([grad_scale_one, grad_scale_two]), jnp.stack([grad_shift_one, grad_shift_two])),
        ("dp", "blk", "tensor"),
    )
    return (
        result,
        grad_input,
        weight_sums[0],
        weight_sums[1],
        weight_sums[2],
        weight_sums[3],
        norm_sums[0],
        norm_sums[1],
    )


def solution(mesh):
    placed = (
        P(("blk", "tensor"), "dp", None),
        P(("blk", "tensor"), "dp", None),
        P(),
        P(),
        P(None, None, "tensor"),
        P("tensor", None),
        P(None, None, "tensor"),
        P("tensor", None),
        P("dp"),
    )
    return jax.shard_map(
        shards,
        mesh=mesh,
        in_specs=placed,
        out_specs=(
            P(("blk", "tensor"), "dp", None),
            P(("blk", "tensor"), "dp", None),
            P(None, None, "tensor"),
            P("tensor", None),
            P(None, None, "tensor"),
            P("tensor", None),
            P(),
            P(),
        ),
        check_vma=False,
    )
```

profile of v0, /device:TPU:1, one launch (start us, length us, event | category | flops | bytes accessed | tf_op | source)
XLA Modules:
  0.0 955.3 jit_solution(10844713691218219755)
XLA Ops:
  11.9 2.0 fusion.48
  15.0 73.5 %all-gather.8.cloned.1.call-done = bf16[512,3,1024]{2,0,1:T(8,128)(2,1)} async-done(((bf16[64,3,1024]{2,0,1:T(8,128)(2,1)}), bf16[512,3,1024]{2,0,1:T(8,128)(2,1)}) %all-gather.8.cloned.1.call-update) | async-done | bytes 3145744 | tf_op jit(solution)/shard_map/all_gather | solution.py:120
  88.5 3.5 fusion.17
  98.7 22.4 %all-gather.10.cloned.1.call-done = bf16[2048,3,128]{0,2,1:T(8,128)(2,1)} async-done(((bf16[512,3,128]{0,2,1:T(8,128)(2,1)}), bf16[2048,3,128]{0,2,1:T(8,128)(2,1)}) %all-gather.10.cloned.1.call-update) | async-done | bytes 1572880 | tf_op jit(solution)/shard_map/all_gather | solution.py:133
  122.7 2.3 fusion.4
  131.5 2.1 copy-done.3
  138.9 11.2 %all-gather.18.cloned.1.call-done = bf16[1,2048,3,128]{1,3,0,2:T(8,128)(2,1)} async-done(((bf16[1,512,3,128]{1,3,0,2:T(8,128)(2,1)}), bf16[1,2048,3,128]{1,3,0,2:T(8,128)(2,1)}) %all-gather.18.cloned.1.call-update) | async-done | bytes 1572880 | tf_op jit(solution)/shard_map/all_gather | solution.py:134
  151.8 4.4 fusion.88
  158.0 2.0 convolution_add_fusion.5
  160.0 2.0 convolution_add_fusion.4
  162.1 2.5 fusion.117
  164.6 2.7 convolution_convert_fusion
  167.3 71.7 %reduce-scatter.7.cloned.1.call-done = bf16[64,3,1024]{2,0,1:T(8,128)(2,1)} async-done(((bf16[512,3,1024]{2,0,1:T(8,128)(2,1)}), bf16[64,3,1024]{2,0,1:T(8,128)(2,1)}) %reduce-scatter.7.cloned.1.call-update) | async-done | bytes 393232 | tf_op jit(solution)/shard_map/reduce_scatter | solution.py:156
  244.6 70.0 %all-gather.12.cloned.1.call-done = bf16[512,3,1024]{2,0,1:T(8,128)(2,1)} async-done(((bf16[64,3,1024]{2,0,1:T(8,128)(2,1)}), bf16[512,3,1024]{2,0,1:T(8,128)(2,1)}) %all-gather.12.cloned.1.call-update) | async-done | bytes 3145744 | tf_op jit(solution)/shard_map/all_gather | solution.py:166
  314.6 8.7 fusion.13
  323.3 63.9 %all-gather.14.cloned.1.call-done = bf16[512,3,1024]{2,0,1:T(8,128)(2,1)} async-done(((bf16[64,3,1024]{2,0,1:T(8,128)(2,1)}), bf16[512,3,1024]{2,0,1:T(8,128)(2,1)}) %all-gather.14.cloned.1.call-update) | async-done | bytes 3145744 | tf_op jit(solution)/shard_map/all_gather | solution.py:183
  387.2 6.9 multiply_convert_fusion.4
  396.0 3.6 add_convert_fusion.1
  399.6 71.6 %reduce-scatter.11.cloned.1.call-done = bf16[64,3,1024]{2,0,1:T(8,128)(2,1)} async-done(((bf16[512,3,1024]{2,0,1:T(8,128)(2,1)}), bf16[64,3,1024]{2,0,1:T(8,128)(2,1)}) %reduce-scatter.11.cloned.1.call-update) | async-done | bytes 393232 | tf_op jit(solution)/shard_map/reduce_scatter | solution.py:195
  473.8 2.1 fusion.52
  476.5 2.2 fusion.64
  479.0 4.3 fusion.21
  486.7 63.2 %all-gather.16.cloned.1.call-done = bf16[512,3,1024]{2,0,1:T(8,128)(2,1)} async-done(((bf16[64,3,1024]{2,0,1:T(8,128)(2,1)}), bf16[512,3,1024]{2,0,1:T(8,128)(2,1)}) %all-gather.16.cloned.1.call-update) | async-done | bytes 3145744 | tf_op jit(solution)/shard_map/all_gather | solution.py:210
  549.9 3.5 multiply_reduce_fusion
  553.5 4.5 multiply_convert_fusion.1
  558.1 2.5 multiply_convert_fusion.2
  560.9 2.4 multiply_convert_fusion.3
  563.9 2.4 multiply_convert_fusion
  574.8 5.2 bitcast_convert_fusion
  580.1 4.4 fusion.80
  585.4 4.4 fusion.83
  590.8 4.5 fusion.86
  596.2 5.3 fusion.77
  601.5 2.0 copy.45
  603.5 2.4 dynamic_update_slice.28
  610.3 3.4 fusion.118
  614.0 2.9 convolution_add_fusion.2
  628.7 10.2 %reduce-scatter.15.cloned.1.call-done = bf16[512,3,128]{2,0,1:T(8,128)(2,1)} async-done(((bf16[2048,3,128]{2,0,1:T(8,128)(2,1)}), bf16[512,3,128]{2,0,1:T(8,128)(2,1)}) %reduce-scatter.15.cloned.1.call-update) | async-done | bytes 393232 | tf_op jit(solution)/shard_map/reduce_scatter | solution.py:245
  638.8 3.0 fusion.32
  645.3 2.7 add_convert_fusion
  648.1 4.9 convolution_convert_fusion.1
  652.9 141.2 %all-reduce.6.cloned.1.call-done = (bf16[3,1024,128]{2,1,0:T(8,128)(2,1)}, bf16[128,1024]{1,0:T(8,128)(2,1)}, bf16[2,1024,512]{2,1,0:T(8,128)(2,1)}, bf16[512,1024]{1,0:T(8,128)(2,1)}) async-done(((bf16[3,1024,128]{2,1,0:T(8,128)(2,1)}, bf16[128,1024]{1,0:T(8,128)(2,1)}, bf16[2,1024,512]{2,1,0:T(8,128)(2,1)}, bf16[512,1024]{1,0:T(8,128)(2,1)}), (bf16[3,1024,128]{2,1,0:T(8,128)(2,1)}, ...) | async-done | bytes 4194320 | tf_op jit(solution)/shard_map/psum | solution.py:284
  796.1 2.4 convert_element_type.193
  800.1 2.6 convert_element_type.196
  802.7 68.0 %reduce-scatter.17.cloned.1.call-done = bf16[64,3,1024]{2,0,1:T(8,128)(2,1)} async-done(((bf16[512,3,1024]{2,0,1:T(8,128)(2,1)}), bf16[64,3,1024]{2,0,1:T(8,128)(2,1)}) %reduce-scatter.17.cloned.1.call-update) | async-done | bytes 393232 | tf_op jit(solution)/shard_map/reduce_scatter | solution.py:267
  873.5 66.8 %all-reduce.2 = (f32[2,1024]{1,0:T(2,128)}, f32[2,1024]{1,0:T(2,128)}) all-reduce(f32[2,1024]{1,0:T(2,128)S(1)} %pad_maximum_fusion.5, f32[2,1024]{1,0:T(2,128)S(1)} %pad_maximum_fusion.6), channel_id=1, replica_groups=mesh['dp'=4,'blk'=4,'tensor'=8] {'dp','blk','tensor'}, use_global_device_ids=true, to_apply=%region_29.30 | all-reduce | flops 4096 | bytes 32768 | tf_op jit(solution)/shard_map/psum | solution.py:289
  940.3 5.5 reduce-scatter.9.cloned.1.call-done
  945.9 2.6 add_convert_fusion.2
  (295 shorter events, 81.4 us)
Async XLA Ops:
  7.2 380.0 %copy-start = (bf16[512,1024]{1,0:T(8,128)(2,1)S(1)}, bf16[512,1024]{1,0:T(8,128)(2,1)}, u32[]{:S(2)}) copy-start(bf16[512,1024]{1,0:T(8,128)(2,1)} %param.16) | copy-start | bytes 3145732
  7.2 81.3 %all-gather.8.cloned.1.call-start = ((), (), s32[]{:S(2)}) async-start(), calls=%async_computation.6 | async-start | bytes 3538944 | tf_op jit(solution)/shard_map/all_gather | solution.py:120
  9.7 82.3 %copy-start.63 = (f32[64,3]{0,1:T(4,128)}, f32[64,3]{0,1:T(4,128)S(1)}, u32[]{:S(2)}) copy-start(f32[64,3]{0,1:T(4,128)S(1)} %fusion.90) | copy-start | bytes 2308
  13.9 107.3 %all-gather.10.cloned.1.call-start = ((), (), s32[]{:S(2)}) async-start(), calls=%async_computation.7 | async-start | bytes 1966080 | tf_op jit(solution)/shard_map/all_gather | solution.py:133
  15.0 77.3 %copy-start.32 = (f32[512,64]{0,1:T(8,128)}, f32[512,64]{0,1:T(8,128)S(1)}, u32[]{:S(2)}) copy-start(f32[512,64]{0,1:T(8,128)S(1)} %get-tuple-element.51) | copy-start | bytes 393220
  15.0 82.6 %copy-start.25 = (f32[512,64]{0,1:T(8,128)}, f32[512,64]{0,1:T(8,128)S(1)}, u32[]{:S(2)}) copy-start(f32[512,64]{0,1:T(8,128)S(1)} %get-tuple-element.50) | copy-start | bytes 393220
  92.3 6.4 copy-start.20
  94.4 55.7 %all-gather.18.cloned.1.call-start = ((), (), s32[]{:S(2)}) async-start(), calls=%async_computation.17 | async-start | bytes 1966080 | tf_op jit(solution)/shard_map/all_gather | solution.py:134
  95.2 66.8 %copy-start.50 = (pred[3,512]{1,0:T(4,128)(4,1)}, pred[3,512]{1,0:T(4,128)(4,1)S(1)}, u32[]{:S(2)}) copy-start(pred[3,512]{1,0:T(4,128)(4,1)S(1)} %get-tuple-element.60) | copy-start | bytes 4612
  97.2 141.8 %reduce-scatter.7.cloned.1.call-start = ((), (), s32[]{:S(2)}) async-start(), calls=%async_computation.8 | async-start | bytes 3538944 | tf_op jit(solution)/shard_map/reduce_scatter | solution.py:156
  126.7 10.0 %copy-start.4 = (f32[3,2,512,512]{2,3,1,0:T(8,128)}, f32[3,2,512,512]{2,3,1,0:T(8,128)S(1)}, u32[]{:S(2)}) copy-start(f32[3,2,512,512]{2,3,1,0:T(8,128)S(1)} %get-tuple-element.66) | copy-start | bytes 18874372
  128.3 6.8 copy-start.5
  150.1 6.1 slice-start.6
  150.1 6.2 copy-start.55
  150.1 6.2 copy-start.74
  151.8 8.2 copy-start.44
  151.8 10.3 %copy-start.38 = (bf16[1,512,3,128]{1,3,0,2:T(8,128)(2,1)}, bf16[1,512,3,128]{1,3,0,2:T(8,128)(2,1)S(1)}, u32[]{:S(2)}) copy-start(bf16[1,512,3,128]{1,3,0,2:T(8,128)(2,1)S(1)} %get-tuple-element.30) | copy-start | bytes 1179652
  151.8 6.2 slice-start.7
  151.8 8.2 copy-start.6
  164.6 74.4 %copy-start.1 = (bf16[64,3,1024]{2,0,1:T(8,128)(2,1)S(1)}, bf16[64,3,1024]{2,0,1:T(8,128)(2,1)}, u32[]{:S(2)}) copy-start(bf16[64,3,1024]{2,0,1:T(8,128)(2,1)} %param.9) | copy-start | bytes 1179652
  167.3 147.3 %all-gather.12.cloned.1.call-start = ((), (), s32[]{:S(2)}) async-start(), calls=%async_computation.9 | async-start | bytes 3538944 | tf_op jit(solution)/shard_map/all_gather | solution.py:166
  241.5 81.8 %copy-start.69 = (f32[64,3]{0,1:T(4,128)}, f32[64,3]{0,1:T(4,128)S(1)}, u32[]{:S(2)}) copy-start(f32[64,3]{0,1:T(4,128)S(1)} %multiply_reduce_fusion.1) | copy-start | bytes 2308
  241.5 81.8 %copy-start.61 = (f32[64,3]{0,1:T(4,128)}, f32[64,3]{0,1:T(4,128)S(1)}, u32[]{:S(2)}) copy-start(f32[64,3]{0,1:T(4,128)S(1)} %fusion.91) | copy-start | bytes 2308
  243.5 143.7 %all-gather.14.cloned.1.call-start = ((), (), s32[]{:S(2)}) async-start(), calls=%async_computation.11 | async-start | bytes 3538944 | tf_op jit(solution)/shard_map/all_gather | solution.py:183
  244.0 227.2 %reduce-scatter.11.cloned.1.call-start = ((), (), s32[]{:S(2)}) async-start(), calls=%async_computation.12 | async-start | bytes 3538944 | tf_op jit(solution)/shard_map/reduce_scatter | solution.py:195
  387.2 6.9 copy-start.36
  399.5 71.7 %copy-start.7 = (bf16[64,3,1024]{2,0,1:T(8,128)(2,1)S(1)}, bf16[64,3,1024]{2,0,1:T(8,128)(2,1)}, u32[]{:S(2)}) copy-start(bf16[64,3,1024]{2,0,1:T(8,128)(2,1)} %reduce-scatter.7.cloned.1.call-done) | copy-start | bytes 1179652
  399.5 150.3 %all-gather.16.cloned.1.call-start = ((), (), s32[]{:S(2)}) async-start(), calls=%async_computation.13 | async-start | bytes 3538944 | tf_op jit(solution)/shard_map/all_gather | solution.py:210
  478.7 143.6 %reduce-scatter.13.cloned.1.call-start = ((), (), s32[]{:S(2)}) async-start(), calls=%async_computation.14 | async-start | bytes 1966080 | tf_op jit(solution)/shard_map/reduce_scatter | solution.py:242
  549.9 8.1 slice-start.8
  553.4 9.9 %copy-start.47 = (bf16[512,3,128]{0,2,1:T(8,128)(2,1)}, bf16[512,3,128]{0,2,1:T(8,128)(2,1)S(1)}, u32[]{:S(2)}) copy-start(bf16[512,3,128]{0,2,1:T(8,128)(2,1)S(1)} %get-tuple-element.72) | copy-start | bytes 1179652
  553.5 7.0 slice-start
  558.0 8.3 copy-start.11
  560.8 6.6 copy-start.13
  574.5 64.3 %reduce-scatter.15.cloned.1.call-start = ((), (), s32[]{:S(2)}) async-start(), calls=%async_computation.15 | async-start | bytes 1966080 | tf_op jit(solution)/shard_map/reduce_scatter | solution.py:245
  601.5 8.8 copy-start.17
  613.7 180.4 %all-reduce.6.cloned.1.call-start = ((), (), s32[]{:S(2)}) async-start(), calls=%async_computation.18 | async-start | bytes 8388608 | tf_op jit(solution)/shard_map/psum | solution.py:284
  642.9 227.9 %reduce-scatter.17.cloned.1.call-start = ((), (), s32[]{:S(2)}) async-start(), calls=%async_computation.16 | async-start | bytes 3538944 | tf_op jit(solution)/shard_map/reduce_scatter | solution.py:267
  648.0 297.9 %reduce-scatter.9.cloned.1.call-start = ((), (), s32[]{:S(2)}) async-start(), calls=%async_computation.10 | async-start | bytes 3538944 | tf_op jit(solution)/shard_map/reduce_scatter | solution.py:174
  800.0 72.0 %copy-start.73 = (f32[1024]{0:T(1024)S(1)}, f32[1024]{0:T(1024)}, u32[]{:S(2)}) copy-start(f32[1024]{0:T(1024)} %get-tuple-element.14) | copy-start | bytes 12292
  800.0 72.0 %copy-start.68 = (f32[64,3]{0,1:T(4,128)S(1)}, f32[64,3]{0,1:T(4,128)}, u32[]{:S(2)}) copy-start(f32[64,3]{0,1:T(4,128)} %copy-done.67) | copy-start | bytes 2308
  800.0 72.0 %copy-start.64 = (f32[64,3]{0,1:T(4,128)S(1)}, f32[64,3]{0,1:T(4,128)}, u32[]{:S(2)}) copy-start(f32[64,3]{0,1:T(4,128)} %copy-done.63) | copy-start | bytes 2308
  800.0 73.5 %copy-start.72 = (f32[1024]{0:T(1024)S(1)}, f32[1024]{0:T(1024)}, u32[]{:S(2)}) copy-start(f32[1024]{0:T(1024)} %get-tuple-element.8) | copy-start | bytes 12292
  800.0 145.8 %copy-start.15 = (bf16[64,3,1024]{2,0,1:T(8,128)(2,1)S(1)}, bf16[64,3,1024]{2,0,1:T(8,128)(2,1)}, u32[]{:S(2)}) copy-start(bf16[64,3,1024]{2,0,1:T(8,128)(2,1)} %reduce-scatter.11.cloned.1.call-done) | copy-start | bytes 1179652
  800.0 145.8 %copy-start.18 = (bf16[64,3,1024]{2,0,1:T(8,128)(2,1)S(1)}, bf16[64,3,1024]{2,0,1:T(8,128)(2,1)}, u32[]{:S(2)}) copy-start(bf16[64,3,1024]{2,0,1:T(8,128)(2,1)} %param.10) | copy-start | bytes 1179652
  800.1 145.8 %copy-start.62 = (f32[64,3]{0,1:T(4,128)S(1)}, f32[64,3]{0,1:T(4,128)}, u32[]{:S(2)}) copy-start(f32[64,3]{0,1:T(4,128)} %copy-done.61) | copy-start | bytes 2308
  800.1 145.8 %copy-start.66 = (f32[64,3]{0,1:T(4,128)S(1)}, f32[64,3]{0,1:T(4,128)}, u32[]{:S(2)}) copy-start(f32[64,3]{0,1:T(4,128)} %copy-done.65) | copy-start | bytes 2308
  800.1 145.8 %copy-start.71 = (f32[64,3]{0,1:T(4,128)S(1)}, f32[64,3]{0,1:T(4,128)}, u32[]{:S(2)}) copy-start(f32[64,3]{0,1:T(4,128)} %copy-done.70) | copy-start | bytes 2308
  (57 other events, 178.8 us)
Sparse Core Ops, SparseCore 0:
  14.0 74.4 all-gather.7
  94.6 26.5 all-gather.9
  123.4 26.6 all-gather.17
  167.4 71.5 reduce-scatter.6
  243.6 70.9 all-gather.11
  316.1 71.0 all-gather.13
  399.7 71.4 reduce-scatter.10
  478.8 70.9 all-gather.15
  574.7 24.9 reduce-scatter.12
  613.8 24.9 reduce-scatter.14
  643.0 151.1 all-reduce.5
  796.4 74.2 reduce-scatter.16
  873.1 72.6 reduce-scatter.8
where the time goes:
time: 959 us; the launch traced here: 955 us
  waiting for transfers between devices  673 us (70%)
  matrix products  119 us (12%)
  blocking collectives  66.8 us (7%)
  other arithmetic  45.6 us (5%)
  local copies, waits for them, and re-layouts  33.4 us (3%)
  between operations  15.5 us (2%)
    psum x1, waiting for transfers between devices, shards(): lax.psum(grad_qkv.astype(jnp.bfloat16), ('dp', 'blk')).astype(jnp.float32)  141 us
    all_gather x1, waiting for transfers between devices, shards(): rows_one = lax.all_gather(normed_one, 'tensor', axis=0, tiled=True)  73.5 us
    reduce_scatter x1, waiting for transfers between devices, shards(): lax.psum_scatter(jnp.einsum('swe,ed->swd', picked, w_out, preferred_eleme...  71.7 us
    reduce_scatter x1, waiting for transfers between devices, shards(): lax.psum_scatter((jnp.einsum('swf,df->swd', grad_gating, w_gate_up[0], pr...  71.6 us
    all_gather x1, waiting for transfers between devices, shards(): rows_two = lax.all_gather(normed_two, 'tensor', axis=0, tiled=True)  70 us
    reduce_scatter x1, waiting for transfers between devices, shards(): lax.psum_scatter((jnp.einsum('swe,de->swd', grad_query_pre, w_qkv[0], pre...  68 us
    psum x1, blocking collectives, shards(): lax.psum((jnp.stack([grad_scale_one, grad_scale_two]), jnp.stack([grad_sh...  66.8 us
    all_gather x1, waiting for transfers between devices, shards(): grad_rows = lax.all_gather(out_grad, 'tensor', axis=0, tiled=True)  63.9 us
  transfers between devices with their start and end apart: 13, of which 12 were waited for; matrix products, arithmetic and copies ran while one was open for 11% of the time, Pallas kernels for 0%

commit v1 on v0

v1 whole, which is shorter than its diff:
```python
import jax
import jax.numpy as jnp
from jax import lax
from jax.experimental import pallas as pl
from jax.experimental.pallas import tpu as pltpu
from jax.sharding import PartitionSpec as P

HD = 64
EPSILON = 1e-05
MASKED = -1000000000.0
F32 = jnp.float32
BF16 = jnp.bfloat16
VMEM_LIMIT = 48 * 1024 * 1024


def send_y(values, step):
    pairs = [(i, ((i // 2 + step) % 4) * 2 + i % 2) for i in range(8)]
    return lax.ppermute(values, "tensor", pairs)


def send_pair(values):
    return lax.ppermute(values, "tensor", [(i, i ^ 1) for i in range(8)])


def send_z(values, step):
    return lax.ppermute(values, "blk", [(i, (i + step) % 4) for i in range(4)])


def send_core(values):
    return lax.ppermute(values, "dp", [(i, i ^ 1) for i in range(4)])


def send_far(values):
    return lax.ppermute(values, "dp", [(i, i ^ 2) for i in range(4)])


def send_x(values, steps):
    pairs = []
    for d in range(4):
        for t in range(8):
            core = d % 2
            x = ((d // 2) * 2 + t % 2 + steps[core]) % 4
            pairs.append((d * 8 + t, ((x // 2) * 2 + core) * 8 + (t // 2) * 2 + x % 2))
    return lax.ppermute(values, ("dp", "tensor"), pairs)


def gather_y(values):
    return [values] + [send_y(values, -r) for r in (1, 2, 3)]


def scatter_y(total):
    rows = total.shape[0] // 4
    parts = [lax.slice_in_dim(total, r * rows, (r + 1) * rows, axis=0) for r in range(4)]
    out = parts[0].astype(F32)
    for r in (1, 2, 3):
        out = out + send_y(parts[r], r).astype(F32)
    return out


def norm_parts(values):
    mean = jnp.mean(values, axis=-1, keepdims=True)
    centred = values - mean
    inverse = lax.rsqrt(jnp.mean(centred * centred, axis=-1, keepdims=True) + EPSILON)
    return centred * inverse, inverse


def norm_back(normed, inverse, gain, cotangent):
    e = cotangent * gain
    grad = (
        e
        - jnp.mean(e, axis=-1, keepdims=True)
        - normed * jnp.mean(e * normed, axis=-1, keepdims=True)
    ) * inverse
    return grad, jnp.sum(cotangent * normed, axis=0), jnp.sum(cotangent, axis=0)


def dot(a, b, ca, cb):
    return lax.dot_general(a, b, (((ca,), (cb,)), ((), ())), preferred_element_type=F32)


def load_keys(own, pair, bias):
    keys = jnp.concatenate([r[:HD, :] for r in own + pair], axis=1)
    values = jnp.concatenate([r[HD:, :] for r in own + pair], axis=1)
    row = lax.broadcasted_iota(jnp.int32, (16, keys.shape[1]), 0)
    extra = jnp.where(row == 0, bias[...], 0.0).astype(BF16)
    return keys, values, jnp.concatenate([keys, extra], axis=0)


def with_one(queries):
    row = lax.broadcasted_iota(jnp.int32, (16, queries.shape[1]), 0)
    return jnp.concatenate([queries, jnp.where(row == 0, 1.0, 0.0).astype(BF16)], axis=0)


def attend_kernel(*refs):
    q, own, pair, bias = refs[0:4], refs[4:8], refs[8:12], refs[12]
    out, wide, lse = refs[13:17], refs[17], refs[18]
    _, values, keys_bias = load_keys(own, pair, bias)
    keys_rows = keys_bias.T
    for i in range(4):
        scores = dot(keys_rows, with_one(q[i][...]), 1, 0)
        top = jnp.max(scores, axis=0, keepdims=True)
        weights = jnp.exp(scores - top)
        total = jnp.sum(weights, axis=0, keepdims=True)
        attended = dot(values, weights.astype(BF16), 1, 0) * (1.0 / total)
        wide[i] = attended
        out[i][...] = attended.astype(BF16)
        lse[i] = top + jnp.log(total)


def attend_back_kernel(*refs):
    q, own, pair, bias = refs[0:4], refs[4:8], refs[8:12], refs[12]
    dob, wide, lse = refs[13:17], refs[17], refs[18]
    dq, d_own, d_pair = refs[19:23], refs[23:27], refs[27:31]
    keys, values, keys_bias = load_keys(own, pair, bias)
    keys_rows = keys_bias.T
    values_rows = values.T
    dk = jnp.zeros((keys.shape[1], HD), F32)
    dv = jnp.zeros((keys.shape[1], HD), F32)
    for i in range(4):
        queries, grad = q[i][...], dob[i][...]
        scores = dot(keys_rows, with_one(queries), 1, 0)
        weights = jnp.exp(scores - lse[i])
        delta = jnp.sum(grad.astype(F32) * wide[i], axis=0, keepdims=True)
        grad_weights = dot(values_rows, grad, 1, 0)
        grad_scores = (weights * (grad_weights - delta)).astype(BF16)
        dq[i][...] = (dot(keys, grad_scores, 1, 0) * 0.125).astype(BF16)
        dk = dk + dot(grad_scores, queries, 1, 1)
        dv = dv + dot(weights.astype(BF16), grad, 1, 1)
    dkv = jnp.concatenate([dk, dv], axis=1).T
    width = q[0].shape[1]
    for i, ref in enumerate(d_own + d_pair):
        ref[...] = dkv[:, i * width : (i + 1) * width].astype(BF16)


def attend(q, own, pair, bias):
    width = q[0].shape[1]
    piece = jax.ShapeDtypeStruct((HD, width), BF16)
    out = pl.pallas_call(
        attend_kernel,
        out_shape=[piece] * 4
        + [jax.ShapeDtypeStruct((4, HD, width), F32), jax.ShapeDtypeStruct((4, 1, width), F32)],
        compiler_params=pltpu.CompilerParams(vmem_limit_bytes=VMEM_LIMIT),
        cost_estimate=pl.CostEstimate(
            flops=4 * 4 * width * 8 * width * HD, bytes_accessed=3_000_000, transcendentals=0
        ),
        name="attend",
    )(*q, *own, *pair, bias)
    return list(out[:4]), out[4], out[5]


def attend_back(q, own, pair, bias, dob, wide, lse):
    width = q[0].shape[1]
    piece = jax.ShapeDtypeStruct((HD, width), BF16)
    double = jax.ShapeDtypeStruct((2 * HD, width), BF16)
    out = pl.pallas_call(
        attend_back_kernel,
        out_shape=[piece] * 4 + [double] * 8,
        compiler_params=pltpu.CompilerParams(vmem_limit_bytes=VMEM_LIMIT),
        cost_estimate=pl.CostEstimate(
            flops=10 * 4 * width * 8 * width * HD, bytes_accessed=3_000_000, transcendentals=0
        ),
        name="attend_back",
    )(*q, *own, *pair, bias, *dob, wide, lse)
    return list(out[:4]), list(out[4:8]), list(out[8:12])


def pick(values, index, size=1, axis=0):
    return lax.dynamic_slice_in_dim(values, index, size, axis)


def sum_over_copies(grads, z):
    out = []
    for grad in grads:
        rows = grad.shape[0] // 4
        part = pick(grad, z * rows, rows).astype(F32)
        for r in (1, 2, 3):
            part = part + send_z(pick(grad, ((z + r) % 4) * rows, rows), r).astype(F32)
        low = part.astype(BF16)
        low = (low.astype(F32) + send_far(low).astype(F32)).astype(BF16)
        ring = [low] + [send_z(low, -r) for r in (1, 2, 3)]
        ring = jnp.concatenate(ring + ring, axis=0)
        out.append(pick(ring, ((4 - z) % 4) * rows, 4 * rows))
    return out


def shards(hidden_in, out_grad, norm_scales, norm_shifts, w_qkv, w_out, w_gate_up, w_down, lengths):
    rows, windows, width = hidden_in.shape
    tensor = lax.axis_index("tensor")
    y, xl = tensor // 2, tensor % 2
    z = lax.axis_index("blk")
    core = lax.axis_index("dp") % 2
    tokens = 4 * rows
    ff = w_down.shape[0]
    half = ff // 2

    x_own = [hidden_in[:, w, :] for w in range(windows)]
    dy_own = [out_grad[:, w, :] for w in range(windows)]
    x_all = [jnp.concatenate(gather_y(v), axis=0) for v in x_own]

    heads_own = jnp.concatenate(
        [
            w_qkv.reshape(3, width, 2, HD).transpose(2, 0, 3, 1).reshape(2, 3 * HD, width),
            w_out.reshape(2, HD, width),
        ],
        axis=1,
    )
    heads_recv = send_x(pick(heads_own, core), (-1, 1))
    heads_four = jnp.concatenate([heads_own, heads_recv, send_core(heads_recv)], axis=0)
    gate_up_recv = send_x(pick(w_gate_up, core * half, half, 2), (-1, 1))
    down_recv = send_x(pick(w_down, core * half, half, 0), (-1, 1))
    w_gu = jnp.concatenate([w_gate_up, gate_up_recv, send_core(gate_up_recv)], axis=2)
    w_gu = jnp.concatenate([w_gu[0], w_gu[1]], axis=1)
    w_d = jnp.concatenate([w_down, down_recv, send_core(down_recv)], axis=0)

    heads_rel = []
    for r in range(4):
        head = (z + r) % 4
        place = jnp.where(head // 2 == xl, head % 2, 2 + ((head % 2) ^ core))
        heads_rel.append(pick(heads_four, place))
    heads_rel = jnp.concatenate(heads_rel, axis=0)
    w_in = heads_rel[:, : 3 * HD].reshape(12 * HD, width)
    w_back = heads_rel[:, 3 * HD :].reshape(4 * HD, width)

    dy_all = [jnp.concatenate(gather_y(v), axis=0) for v in dy_own]

    lane = jnp.arange(tokens, dtype=jnp.int32)
    within = ((y + lane // rows) % 4) * (2 * rows) + lane % rows
    inverse = 10000.0 ** (-(jnp.arange(HD // 2, dtype=F32) * 2.0) / HD)
    angles = inverse[:, None] * (z * (8 * rows) + within + xl * rows).astype(F32)[None, :]
    cosine, sine = jnp.cos(angles), jnp.sin(angles)
    key_places = jnp.concatenate(
        [
            ((z - r) % 4) * (8 * rows) + within + side * rows
            for side in (xl, 1 - xl)
            for r in range(4)
        ]
    )
    bias = [
        jnp.where(key_places < lengths[w], 0.0, MASKED).astype(F32)[None, :] for w in range(windows)
    ]

    saved = []
    for w in range(windows):
        normed, _ = norm_parts(x_all[w].astype(F32))
        h1 = (normed * norm_scales[0] + norm_shifts[0]).astype(BF16)
        proj = dot(w_in, h1, 1, 1).reshape(4, 3, 2, HD // 2, tokens)
        first, second = proj[:, :2, 0], proj[:, :2, 1]
        turned = jnp.stack([first * cosine - second * sine, second * cosine + first * sine], axis=2)
        q_send = (turned[:, 0] * 0.125).astype(BF16).reshape(4, HD, tokens)
        kv_send = jnp.stack([turned[:, 1], proj[:, 2]], axis=1).astype(BF16)
        kv_send = kv_send.reshape(4, 2 * HD, tokens)
        q = [q_send[0]] + [send_z(q_send[r], r) for r in (1, 2, 3)]
        own = [kv_send[0]] + [send_z(kv_send[r], r) for r in (1, 2, 3)]
        pair = [send_pair(v) for v in own]
        out, wide, lse = attend(q, own, pair, bias[w])
        ob = jnp.concatenate([out[0]] + [send_z(out[r], -r) for r in (1, 2, 3)], axis=0)
        attn = scatter_y(dot(ob, w_back, 0, 0).astype(BF16))
        middle = x_own[w].astype(F32) + attn
        saved.append((h1, q, own, pair, wide, lse, ob, middle))

    ffn = []
    for w in range(windows):
        middle = saved[w][7]
        normed, inv = norm_parts(middle)
        h2 = jnp.concatenate(
            gather_y((normed * norm_scales[1] + norm_shifts[1]).astype(BF16)), axis=0
        )
        gate_up = dot(h2, w_gu, 1, 0)
        gate, up = gate_up[:, : 2 * ff], gate_up[:, 2 * ff :]
        sig = jax.nn.sigmoid(gate)
        act = gate * sig
        hid = (act * up).astype(BF16)
        dh = dot(dy_all[w], w_d, 1, 1)
        d_gate = (dh * up * (sig * (1.0 + gate * (1.0 - sig)))).astype(BF16)
        d_up = (dh * act).astype(BF16)
        d_gu = jnp.concatenate([d_gate, d_up], axis=1)
        dh2 = scatter_y(dot(d_gu, w_gu, 1, 1).astype(BF16))
        y_out = scatter_y(dot(hid, w_d, 1, 0).astype(BF16))
        result = (middle + y_out).astype(BF16)
        back, g_scale, g_shift = norm_back(normed, inv, norm_scales[1], dh2)
        dx2 = dy_own[w].astype(F32) + back
        ffn.append((h2, hid, d_gu, result, dx2, g_scale, g_shift))

    g_d = sum(dot(ffn[w][1], dy_all[w], 0, 0) for w in range(windows)).astype(BF16)
    g_gu = sum(dot(ffn[w][0], ffn[w][2], 0, 0) for w in range(windows)).astype(BF16)
    g_g, g_u = g_gu[:, : 2 * ff], g_gu[:, 2 * ff :]

    def own_half(values, which, axis):
        return pick(lax.slice_in_dim(values, 0, ff, axis=axis), which * half, half, axis)

    def far_half(values, which, axis):
        return lax.slice_in_dim(values, ff + which * half, ff + (which + 1) * half, axis=axis)

    keep_gu = [jnp.concatenate([own_half(g, core, 1) for g in (g_g, g_u)], axis=1)]
    keep_gu.append(jnp.concatenate([far_half(g, 0, 1) for g in (g_g, g_u)], axis=1))
    give_gu = [jnp.concatenate([own_half(g, 1 - core, 1) for g in (g_g, g_u)], axis=1)]
    give_gu.append(jnp.concatenate([far_half(g, 1, 1) for g in (g_g, g_u)], axis=1))
    keep_d = [own_half(g_d, core, 0), far_half(g_d, 0, 0)]
    give_d = [own_half(g_d, 1 - core, 0), far_half(g_d, 1, 0)]

    def add(a, b):
        return (a.astype(F32) + b.astype(F32)).astype(BF16)

    def fold(keep, give):
        own, far = (add(k, send_core(g)) for k, g in zip(keep, give))
        return add(own, send_x(far, (-1, 1)))

    sum_gu, sum_d = sum_over_copies([fold(keep_gu, give_gu), fold(keep_d, give_d)], z)

    def both(mine, axis):
        other = send_core(mine)
        low = jnp.where(core == 0, mine, other).astype(F32)
        high = jnp.where(core == 0, other, mine).astype(F32)
        return jnp.concatenate([low, high], axis=axis)

    grad_gate_up = jnp.stack([both(sum_gu[:, :half], 1), both(sum_gu[:, half:], 1)])
    grad_down = both(sum_d, 0)

    g_in, g_back = 0.0, 0.0
    grads_in, scales, shifts = [], [], []
    for w in range(windows):
        h1, q, own, pair, wide, lse, ob, _ = saved[w]
        dx2 = ffn[w][4]
        da = jnp.concatenate(gather_y(dx2.astype(BF16)), axis=0)
        g_back = g_back + dot(ob, da, 1, 0)
        dob_send = dot(w_back, da, 1, 1).astype(BF16).reshape(4, HD, tokens)
        dob = [dob_send[0]] + [send_z(dob_send[r], r) for r in (1, 2, 3)]
        dq, d_own, d_pair = attend_back(q, own, pair, bias[w], dob, wide, lse)
        d_kv = [add(a, send_pair(b)) for a, b in zip(d_own, d_pair)]
        dq = [dq[0]] + [send_z(dq[r], -r) for r in (1, 2, 3)]
        d_kv = [d_kv[0]] + [send_z(d_kv[r], -r) for r in (1, 2, 3)]
        pieces = []
        for r in range(4):
            for grad in (dq[r], d_kv[r][:HD]):
                first, second = grad[: HD // 2].astype(F32), grad[HD // 2 :].astype(F32)
                pieces.append((first * cosine + second * sine).astype(BF16))
                pieces.append((second * cosine - first * sine).astype(BF16))
            pieces.append(d_kv[r][HD:])
        d_proj = jnp.concatenate(pieces, axis=0)
        g_in = g_in + dot(d_proj, h1, 1, 0)
        dh1 = scatter_y(dot(d_proj, w_in, 0, 0).astype(BF16))
        normed, inv = norm_parts(x_own[w].astype(F32))
        back, g_scale, g_shift = norm_back(normed, inv, norm_scales[0], dh1)
        grads_in.append((dx2 + back).astype(BF16))
        scales.append(g_scale)
        shifts.append(g_shift)

    g_heads = jnp.concatenate(
        [g_in.reshape(4, 3 * HD, width), g_back.reshape(4, HD, width)], axis=1
    ).astype(BF16)

    def head_at(head):
        return pick(g_heads, (head - z) % 4)[0]

    keep = [head_at(2 * xl + core), head_at(2 * (1 - xl) + core)]
    give = [head_at(2 * xl + 1 - core), head_at(2 * (1 - xl) + 1 - core)]
    (sum_heads,) = sum_over_copies([fold(keep, give)], z)
    heads = both(sum_heads[None], 0)
    grad_qkv = heads[:, : 3 * HD].reshape(2, 3, HD, width).transpose(1, 3, 0, 2)
    grad_qkv = grad_qkv.reshape(3, width, 2 * HD)
    grad_out = heads[:, 3 * HD :].reshape(2 * HD, width)

    small = jnp.stack([sum(scales), sum(f[5] for f in ffn), sum(shifts), sum(f[6] for f in ffn)])
    small = small + send_core(small)
    small = small + sum(send_y(small, r) for r in (1, 2, 3))
    small = small + sum(send_x(small, (r, r)) for r in (1, 2, 3))
    small = small + sum(send_z(small, r) for r in (1, 2, 3))

    return (
        jnp.stack([f[3] for f in ffn], axis=1),
        jnp.stack(grads_in, axis=1),
        grad_qkv,
        grad_out,
        grad_gate_up,
        grad_down,
        small[:2],
        small[2:],
    )


def solution(mesh):
    placed = (
        P(("blk", "tensor"), "dp", None),
        P(("blk", "tensor"), "dp", None),
        P(),
        P(),
        P(None, None, "tensor"),
        P("tensor", None),
        P(None, None, "tensor"),
        P("tensor", None),
        P("dp"),
    )
    return jax.shard_map(
        shards,
        mesh=mesh,
        in_specs=placed,
        out_specs=(
            P(("blk", "tensor"), "dp", None),
            P(("blk", "tensor"), "dp", None),
            P(None, None, "tensor"),
            P("tensor", None),
            P(None, None, "tensor"),
            P("tensor", None),
            P(),
            P(),
        ),
        check_vma=False,
    )
```

time: 959 us -> 553 us (0.58)
  waiting for transfers between devices: 673 us -> 126 us
  starting transfers between devices: 1.99 us -> 285 us
  matrix products: 119 us -> 42.9 us
  blocking collectives: 66.8 us -> 0 us
  Pallas kernels: 0 us -> 31.8 us
  other arithmetic: 45.6 us -> 28.7 us
  between operations: 15.5 us -> 3.95 us
    all_gather x6 -> x0, waiting for transfers between devices: 304 us -> none  [the longest x1 73.5 us: shards(): rows_one = lax.all_gather(normed_one, 'tensor', axis=0, tiled=True)]
    ppermute x0 -> x200, starting transfers between devices: none -> 285 us  [the longest x14 89.4 us: send_core(): return lax.ppermute(values, 'dp', [(i, i ^ 1) for i in range(4)])]
    reduce_scatter x6 -> x0, waiting for transfers between devices: 227 us -> none  [the longest x1 71.7 us: shards(): lax.psum_scatter(jnp.einsum('swe,ed->swd', picked, w_out, preferred_eleme...]
    psum x1 -> x0, waiting for transfers between devices: 141 us -> none  [shards(): lax.psum(grad_qkv.astype(jnp.bfloat16), ('dp', 'blk')).astype(jnp.float32)]
    ppermute x0 -> x200, waiting for transfers between devices: none -> 126 us  [the longest x75 47.2 us: send_z(): return lax.ppermute(values, 'blk', [(i, (i + step) % 4) for i in range(4)])]
    dot_general x42 -> x36, matrix products: 119 us -> 42.9 us  [dot(): lax.dot_general(a, b, (((ca,), (cb,)), ((), ())), preferred_element_type=...]
    psum x1 -> x0, blocking collectives: 66.8 us -> none  [shards(): lax.psum((jnp.stack([grad_scale_one, grad_scale_two]), jnp.stack([grad_sh...]
    pallas_call x0 -> x6, Pallas kernels: none -> 31.8 us  [the longest x3 16.6 us: attend_back(): pl.pallas_call(attend_back_kernel, out_shape=[piece] * 4 + [double] * 8,...]
  transfers between devices with their start and end apart: 13 -> 200, of which waited for: 12 -> 64; matrix products, arithmetic and copies ran while one was open for 11% -> 13% of each run, Pallas kernels for 0% -> 6%
where the time goes in v1:
time: 553 us; the launch traced here: 543 us
  starting transfers between devices  285 us (52%)
  waiting for transfers between devices  126 us (23%)
  matrix products  42.9 us (8%)
  Pallas kernels  31.8 us (6%)
  other arithmetic  28.7 us (5%)
  local copies, waits for them, and re-layouts  24.3 us (4%)
    ppermute x14, starting transfers between devices, send_core(): return lax.ppermute(values, 'dp', [(i, i ^ 1) for i in range(4)])  89.4 us
    ppermute x75, starting transfers between devices, send_z(): return lax.ppermute(values, 'blk', [(i, (i + step) % 4) for i in range(4)])  83.5 us
    ppermute x75, starting transfers between devices, send_y(): return lax.ppermute(values, 'tensor', pairs)  83.1 us
    ppermute x75, waiting for transfers between devices, send_z(): return lax.ppermute(values, 'blk', [(i, (i + step) % 4) for i in range(4)])  47.2 us
    dot_general x36, matrix products, dot(): lax.dot_general(a, b, (((ca,), (cb,)), ((), ())), preferred_element_type=...  42.9 us
    ppermute x24, waiting for transfers between devices, send_pair(): return lax.ppermute(values, 'tensor', [(i, i ^ 1) for i in range(8)])  31.7 us
    ppermute x75, waiting for transfers between devices, send_y(): return lax.ppermute(values, 'tensor', pairs)  28.1 us
    pallas_call x3, Pallas kernels, attend_back(): pl.pallas_call(attend_back_kernel, out_shape=[piece] * 4 + [double] * 8,...  16.6 us
  transfers between devices with their start and end apart: 200, of which 64 were waited for; matrix products, arithmetic and copies ran while one was open for 13% of the time, Pallas kernels for 6%

profile of v1, /device:TPU:1, one launch (start us, length us, event | category | flops | bytes accessed | tf_op | source)
XLA Modules:
  0.0 543.3 jit_solution(11278755181017947136)
XLA Ops:
  34.8 9.1 %collective-permute-done = bf16[1,256,1024]{2,1,0:T(8,128)(2,1)S(1)} collective-permute-done((bf16[1,256,1024]{2,1,0:T(8,128)(2,1)S(1)}, bf16[1,256,1024]{2,1,0:T(8,128)(2,1)S(1)}, u32[]{:S(2)}, u32[]{:S(2)}) %collective-permute-start) | collective-permute-done | bytes 524320 | tf_op jit(solution)/shard_map/ppermute | solution.py:44
  43.9 3.4 collective-permute-start.1
  54.3 3.7 collective-permute-start.60
  76.1 3.0 collective-permute-done.42.refs_10_
  80.3 5.1 attend.4
  93.4 2.7 collective-permute-start.7
  96.1 5.1 attend.5
  109.6 5.1 attend.3
  122.2 4.0 collective-permute-done.17
  145.1 17.7 %collective-permute-start.25 = (bf16[2,1024,256]{2,1,0:T(8,128)(2,1)S(1)}, bf16[2,1024,256]{2,1,0:T(8,128)(2,1)S(1)}, u32[]{:S(2)}, u32[]{:S(2)}) collective-permute-start(bf16[2,1024,256]{2,1,0:T(8,128)(2,1)S(1)} %collective-permute-done.24), channel_id=1, source_target_pairs={{0,32},{32,0},{64,96},{96,64},{1,33},{33,1},{65,97},{97,65},{2,34}... | collective-permute-start | bytes 3145736 | tf_op jit(solution)/shard_map/ppermute | solution.py:30
  164.3 3.2 collective-permute-start.51
  188.8 3.5 collective-permute-done.133
  201.6 3.8 collective-permute-done.81
  210.0 4.6 fusion.26
  214.6 5.0 add_convert_fusion
  221.9 2.7 collective-permute-start.111
  237.9 2.7 collective-permute-start.136
  255.5 11.7 %collective-permute-start.180 = (bf16[256,1024]{1,0:T(8,128)(2,1)S(1)}, bf16[256,1024]{1,0:T(8,128)(2,1)S(1)}, u32[]{:S(2)}, u32[]{:S(2)}) collective-permute-start(bf16[256,1024]{1,0:T(8,128)(2,1)S(1)} %slice.1080), channel_id=1, source_target_pairs={{0,32},{32,0},{64,96},{96,64},{1,33},{33,1},{65,97},{97,65},{2,34}... | collective-permute-start | bytes 1572872 | tf_op jit(solution)/shard_map/ppermute | solution.py:30
  293.9 5.5 %attend_back.4 = (bf16[64,256]{1,0:T(8,128)(2,1)S(1)}, bf16[64,256]{1,0:T(8,128)(2,1)S(1)}, bf16[64,256]{1,0:T(8,128)(2,1)S(1)}, bf16[64,256]{1,0:T(8,128)(2,1)S...) custom-call(bf16[64,256]{1,0:T(8,128)(2,1)S(1)} %bitcast.221, ...), custom_call_target="tpu_custom_call" | custom-call | flops 1342177280 | bytes 3000000 | tf_op jit(solution)/shard_map/attend_back/pallas_call | solution.py:155
  300.9 3.1 collective-permute-start.119
  304.0 5.6 %attend_back.5 = (bf16[64,256]{1,0:T(8,128)(2,1)S(1)}, bf16[64,256]{1,0:T(8,128)(2,1)S(1)}, bf16[64,256]{1,0:T(8,128)(2,1)S(1)}, bf16[64,256]{1,0:T(8,128)(2,1)S...) custom-call(bf16[64,256]{1,0:T(8,128)(2,1)S(1)} %bitcast.219, ...), custom_call_target="tpu_custom_call" | custom-call | flops 1342177280 | bytes 3000000 | tf_op jit(solution)/shard_map/attend_back/pallas_call | solution.py:155
  311.5 5.5 %attend_back.3 = (bf16[64,256]{1,0:T(8,128)(2,1)S(1)}, bf16[64,256]{1,0:T(8,128)(2,1)S(1)}, bf16[64,256]{1,0:T(8,128)(2,1)S(1)}, bf16[64,256]{1,0:T(8,128)(2,1)S...) custom-call(bf16[64,256]{1,0:T(8,128)(2,1)S(1)} %bitcast.217, ...), custom_call_target="tpu_custom_call" | custom-call | flops 1342177280 | bytes 3000000 | tf_op jit(solution)/shard_map/attend_back/pallas_call | solution.py:155
  326.2 3.2 collective-permute-done.145
  329.5 3.4 collective-permute-done.148
  332.9 3.1 collective-permute-done.93
  336.2 2.9 collective-permute-done.151
  339.7 3.3 collective-permute-done.95
  343.0 3.1 collective-permute-done.98
  346.2 3.1 collective-permute-done.101
  373.8 2.7 collective-permute-start.105
  391.4 22.8 %collective-permute-start.179 = (bf16[256,1024]{1,0:T(8,128)(2,1)S(1)}, bf16[256,1024]{1,0:T(8,128)(2,1)S(1)}, u32[]{:S(2)}, u32[]{:S(2)}) collective-permute-start(bf16[256,1024]{1,0:T(8,128)(2,1)S(1)} %copy-done.32), channel_id=1, source_target_pairs={{0,32},{32,0},{64,96},{96,64},{1,33},{33,1},{65,97},{97,65},{2,34}... | collective-permute-start | bytes 1572872 | tf_op jit(solution)/shard_map/ppermute | solution.py:30
  415.6 5.1 collective-permute-start.190
  426.8 3.6 collective-permute-start.196
  431.4 3.0 collective-permute-done.195
  437.3 4.2 collective-permute-start.168
  441.5 2.8 collective-permute-start.157
  456.4 3.3 collective-permute-done.185
  460.1 4.5 collective-permute-start.186
  464.9 5.1 collective-permute-done.186
  471.3 2.7 collective-permute-start.161
  477.4 5.2 collective-permute-done.160
  484.9 3.2 collective-permute-done.162
  489.4 5.1 collective-permute-start.189
  501.2 4.1 collective-permute-done.170
  505.3 4.8 collective-permute-done.171
  512.4 5.1 collective-permute-start.166
  522.9 3.8 collective-permute-done.175
  529.1 6.9 %collective-permute-start.177 = (bf16[1024,256]{1,0:T(8,128)(2,1)}, bf16[1024,256]{1,0:T(8,128)(2,1)}, u32[]{:S(2)}, u32[]{:S(2)}) collective-permute-start(bf16[1024,256]{1,0:T(8,128)(2,1)} %get-tuple-element.204), channel_id=1, source_target_pairs={{0,32},{32,0},{64,96},{96,64},{1,33},{33,1},{65,97},{97,65},{2,34}... | collective-permute-start | bytes 1572872 | tf_op jit(solution)/shard_map/ppermute | solution.py:30
  (806 shorter events, 303.8 us)
Async XLA Ops:
  1.9 18.3 %collective-permute-start.4 = (bf16[64,1024]{1,0:T(8,128)(2,1)S(1)}, bf16[64,1024]{1,0:T(8,128)(2,1)}, u32[]{:S(2)}, u32[]{:S(2)}) collective-permute-start(bf16[64,1024]{1,0:T(8,128)(2,1)S(1)} %get-tuple-element.291), channel_id=1, source_target_pairs={{0,2},{1,3},{2,4},{3,5},{4,6},{5,7},{6,0},{7,1},{8,10},{9,11},{10,... | collective-permute-start | bytes 393224 | tf_op jit(solution)/shard_map/ppermute | solution.py:18
  4.1 17.8 %collective-permute-start.3 = (bf16[64,1024]{1,0:T(8,128)(2,1)S(1)}, bf16[64,1024]{1,0:T(8,128)(2,1)}, u32[]{:S(2)}, u32[]{:S(2)}) collective-permute-start(bf16[64,1024]{1,0:T(8,128)(2,1)S(1)} %get-tuple-element.291), channel_id=1, source_target_pairs={{0,4},{1,5},{2,6},{3,7},{4,0},{5,1},{6,2},{7,3},{8,12},{9,13},{10,... | collective-permute-start | bytes 393224 | tf_op jit(solution)/shard_map/ppermute | solution.py:18
  6.7 15.7 %collective-permute-start.2 = (bf16[64,1024]{1,0:T(8,128)(2,1)S(1)}, bf16[64,1024]{1,0:T(8,128)(2,1)}, u32[]{:S(2)}, u32[]{:S(2)}) collective-permute-start(bf16[64,1024]{1,0:T(8,128)(2,1)S(1)} %get-tuple-element.291), channel_id=1, source_target_pairs={{0,6},{1,7},{2,0},{3,1},{4,2},{5,3},{6,4},{7,5},{8,14},{9,15},{10,... | collective-permute-start | bytes 393224 | tf_op jit(solution)/shard_map/ppermute | solution.py:18
  7.8 19.0 %collective-permute-start.58 = (bf16[64,1024]{1,0:T(8,128)(2,1)S(1)}, bf16[64,1024]{1,0:T(8,128)(2,1)}, u32[]{:S(2)}, u32[]{:S(2)}) collective-permute-start(bf16[64,1024]{1,0:T(8,128)(2,1)S(1)} %get-tuple-element.292), channel_id=1, source_target_pairs={{0,2},{1,3},{2,4},{3,5},{4,6},{5,7},{6,0},{7,1},{8,10},{9,11},{10,... | collective-permute-start | bytes 393224 | tf_op jit(solution)/shard_map/ppermute | solution.py:18
  8.2 20.7 %collective-permute-start.57 = (bf16[64,1024]{1,0:T(8,128)(2,1)S(1)}, bf16[64,1024]{1,0:T(8,128)(2,1)}, u32[]{:S(2)}, u32[]{:S(2)}) collective-permute-start(bf16[64,1024]{1,0:T(8,128)(2,1)S(1)} %get-tuple-element.292), channel_id=1, source_target_pairs={{0,4},{1,5},{2,6},{3,7},{4,0},{5,1},{6,2},{7,3},{8,12},{9,13},{10,... | collective-permute-start | bytes 393224 | tf_op jit(solution)/shard_map/ppermute | solution.py:18
  28.8 18.8 %collective-permute-start.26 = (bf16[256,1024]{1,0:T(8,128)(2,1)}, bf16[256,1024]{1,0:T(8,128)(2,1)S(1)}, u32[]{:S(2)}, u32[]{:S(2)}) collective-permute-start(bf16[256,1024]{1,0:T(8,128)(2,1)} %constant_dynamic-slice_fusion.15), channel_id=1, source_target_pairs={{0,65},{1,0},{2,67},{3,2},{4,69},{5,4},{6,71},{7,6},{32,33},{33,96... | collective-permute-start | bytes 1572872 | tf_op jit(solution)/shard_map/ppermute | solution.py:44
  33.6 28.3 %collective-permute-start.24 = (bf16[2,1024,256]{2,1,0:T(8,128)(2,1)}, bf16[2,1024,256]{2,1,0:T(8,128)(2,1)S(1)}, u32[]{:S(2)}, u32[]{:S(2)}) collective-permute-start(bf16[2,1024,256]{2,1,0:T(8,128)(2,1)} %constant_dynamic-slice_fusion.16), channel_id=1, source_target_pairs={{0,65},{1,0},{2,67},{3,2},{4,69},{5,4},{6,71},{7,6},{32,33},{33,96... | collective-permute-start | bytes 3145736 | tf_op jit(solution)/shard_map/ppermute | solution.py:44
  70.7 16.2 %collective-permute-start.65 = (bf16[128,256]{1,0:T(8,128)(2,1)S(1)}, bf16[128,256]{1,0:T(8,128)(2,1)S(1)}, u32[]{:S(2)}, u32[]{:S(2)}) collective-permute-start(bf16[128,256]{1,0:T(8,128)(2,1)S(1)} %bitcast.207), channel_id=1, source_target_pairs={{0,1},{1,0},{2,3},{3,2},{4,5},{5,4},{6,7},{7,6},{8,9},{9,8},{10,11... | collective-permute-start | bytes 196616 | tf_op jit(solution)/shard_map/ppermute | solution.py:22
  71.3 15.7 %collective-permute-start.62 = (bf16[128,256]{1,0:T(8,128)(2,1)S(1)}, bf16[128,256]{1,0:T(8,128)(2,1)S(1)}, u32[]{:S(2)}, u32[]{:S(2)}) collective-permute-start(bf16[128,256]{1,0:T(8,128)(2,1)S(1)} %bitcast.275), channel_id=1, source_target_pairs={{0,8},{8,16},{16,24},{24,0},{1,9},{9,17},{17,25},{25,1},{2,10},{10... | collective-permute-start | bytes 196616 | tf_op jit(solution)/shard_map/ppermute | solution.py:26
  73.3 15.7 %collective-permute-start.63 = (bf16[128,256]{1,0:T(8,128)(2,1)S(1)}, bf16[128,256]{1,0:T(8,128)(2,1)S(1)}, u32[]{:S(2)}, u32[]{:S(2)}) collective-permute-start(bf16[128,256]{1,0:T(8,128)(2,1)S(1)} %bitcast.274), channel_id=1, source_target_pairs={{0,16},{8,24},{16,0},{24,8},{1,17},{9,25},{17,1},{25,9},{2,18},{10... | collective-permute-start | bytes 196616 | tf_op jit(solution)/shard_map/ppermute | solution.py:26
  74.6 15.4 %collective-permute-start.68 = (bf16[128,256]{1,0:T(8,128)(2,1)S(1)}, bf16[128,256]{1,0:T(8,128)(2,1)S(1)}, u32[]{:S(2)}, u32[]{:S(2)}) collective-permute-start(bf16[128,256]{1,0:T(8,128)(2,1)S(1)} %collective-permute-done.64.refs_7_), channel_id=1, source_target_pairs={{0,1},{1,0},{2,3},{3,2},{4,5},{5,4},{6,7},{7,6},{8,9},{9,8},{10,11... | collective-permute-start | bytes 196616 | tf_op jit(solution)/shard_map/ppermute | solution.py:22
  85.4 16.6 %collective-permute-start.10 = (bf16[128,256]{1,0:T(8,128)(2,1)S(1)}, bf16[128,256]{1,0:T(8,128)(2,1)S(1)}, u32[]{:S(2)}, u32[]{:S(2)}) collective-permute-start(bf16[128,256]{1,0:T(8,128)(2,1)S(1)} %bitcast.278), channel_id=1, source_target_pairs={{0,24},{8,0},{16,8},{24,16},{1,25},{9,1},{17,9},{25,17},{2,26},{10... | collective-permute-start | bytes 196616 | tf_op jit(solution)/shard_map/ppermute | solution.py:26
  86.9 15.9 %collective-permute-start.8 = (bf16[128,256]{1,0:T(8,128)(2,1)S(1)}, bf16[128,256]{1,0:T(8,128)(2,1)S(1)}, u32[]{:S(2)}, u32[]{:S(2)}) collective-permute-start(bf16[128,256]{1,0:T(8,128)(2,1)S(1)} %bitcast.277), channel_id=1, source_target_pairs={{0,8},{8,16},{16,24},{24,0},{1,9},{9,17},{17,25},{25,1},{2,10},{10... | collective-permute-start | bytes 196616 | tf_op jit(solution)/shard_map/ppermute | solution.py:26
  87.0 16.5 %collective-permute-start.9 = (bf16[128,256]{1,0:T(8,128)(2,1)S(1)}, bf16[128,256]{1,0:T(8,128)(2,1)S(1)}, u32[]{:S(2)}, u32[]{:S(2)}) collective-permute-start(bf16[128,256]{1,0:T(8,128)(2,1)S(1)} %bitcast.276), channel_id=1, source_target_pairs={{0,16},{8,24},{16,0},{24,8},{1,17},{9,25},{17,1},{25,9},{2,18},{10... | collective-permute-start | bytes 196616 | tf_op jit(solution)/shard_map/ppermute | solution.py:26
  105.2 28.4 %collective-permute-start.44 = (bf16[64,256]{1,0:T(8,128)(2,1)S(1)}, bf16[64,256]{1,0:T(8,128)(2,1)S(1)}, u32[]{:S(2)}, u32[]{:S(2)}) collective-permute-start(bf16[64,256]{1,0:T(8,128)(2,1)S(1)} %get-tuple-element.67), channel_id=1, source_target_pairs={{0,24},{8,0},{16,8},{24,16},{1,25},{9,1},{17,9},{25,17},{2,26},{10... | collective-permute-start | bytes 98312 | tf_op jit(solution)/shard_map/ppermute | solution.py:26
  106.9 26.9 %collective-permute-start.45 = (bf16[64,256]{1,0:T(8,128)(2,1)S(1)}, bf16[64,256]{1,0:T(8,128)(2,1)S(1)}, u32[]{:S(2)}, u32[]{:S(2)}) collective-permute-start(bf16[64,256]{1,0:T(8,128)(2,1)S(1)} %get-tuple-element.68), channel_id=1, source_target_pairs={{0,16},{8,24},{16,0},{24,8},{1,17},{9,25},{17,1},{25,9},{2,18},{10... | collective-permute-start | bytes 98312 | tf_op jit(solution)/shard_map/ppermute | solution.py:26
  106.9 27.5 %collective-permute-start.46 = (bf16[64,256]{1,0:T(8,128)(2,1)S(1)}, bf16[64,256]{1,0:T(8,128)(2,1)S(1)}, u32[]{:S(2)}, u32[]{:S(2)}) collective-permute-start(bf16[64,256]{1,0:T(8,128)(2,1)S(1)} %get-tuple-element.69), channel_id=1, source_target_pairs={{0,8},{8,16},{16,24},{24,0},{1,9},{9,17},{17,25},{25,1},{2,10},{10... | collective-permute-start | bytes 98312 | tf_op jit(solution)/shard_map/ppermute | solution.py:26
  107.6 19.8 %collective-permute-start.69 = (bf16[64,256]{1,0:T(8,128)(2,1)S(1)}, bf16[64,256]{1,0:T(8,128)(2,1)S(1)}, u32[]{:S(2)}, u32[]{:S(2)}) collective-permute-start(bf16[64,256]{1,0:T(8,128)(2,1)S(1)} %get-tuple-element.71), channel_id=1, source_target_pairs={{0,24},{8,0},{16,8},{24,16},{1,25},{9,1},{17,9},{25,17},{2,26},{10... | collective-permute-start | bytes 98312 | tf_op jit(solution)/shard_map/ppermute | solution.py:26
  139.1 23.7 %collective-permute-start.49 = (bf16[64,1024]{1,0:T(8,128)(2,1)S(1)}, bf16[64,1024]{1,0:T(8,128)(2,1)S(1)}, u32[]{:S(2)}, u32[]{:S(2)}) collective-permute-start(bf16[64,1024]{1,0:T(8,128)(2,1)S(1)} %get-tuple-element.270), channel_id=1, source_target_pairs={{0,6},{1,7},{2,0},{3,1},{4,2},{5,3},{6,4},{7,5},{8,14},{9,15},{10,... | collective-permute-start | bytes 393224 | tf_op jit(solution)/shard_map/ppermute | solution.py:18
  141.9 21.0 %collective-permute-start.48 = (bf16[64,1024]{1,0:T(8,128)(2,1)S(1)}, bf16[64,1024]{1,0:T(8,128)(2,1)S(1)}, u32[]{:S(2)}, u32[]{:S(2)}) collective-permute-start(bf16[64,1024]{1,0:T(8,128)(2,1)S(1)} %get-tuple-element.271), channel_id=1, source_target_pairs={{0,4},{1,5},{2,6},{3,7},{4,0},{5,1},{6,2},{7,3},{8,12},{9,13},{10,... | collective-permute-start | bytes 393224 | tf_op jit(solution)/shard_map/ppermute | solution.py:18
  142.0 33.8 %collective-permute-start.108 = (bf16[64,1024]{1,0:T(8,128)(2,1)S(1)}, bf16[64,1024]{1,0:T(8,128)(2,1)S(1)}, u32[]{:S(2)}, u32[]{:S(2)}) collective-permute-start(bf16[64,1024]{1,0:T(8,128)(2,1)S(1)} %copy-done.36), channel_id=1, source_target_pairs={{0,2},{1,3},{2,4},{3,5},{4,6},{5,7},{6,0},{7,1},{8,10},{9,11},{10,... | collective-permute-start | bytes 393224 | tf_op jit(solution)/shard_map/ppermute | solution.py:18
  142.6 35.1 %collective-permute-start.107 = (bf16[64,1024]{1,0:T(8,128)(2,1)S(1)}, bf16[64,1024]{1,0:T(8,128)(2,1)S(1)}, u32[]{:S(2)}, u32[]{:S(2)}) collective-permute-start(bf16[64,1024]{1,0:T(8,128)(2,1)S(1)} %copy-done.36), channel_id=1, source_target_pairs={{0,4},{1,5},{2,6},{3,7},{4,0},{5,1},{6,2},{7,3},{8,12},{9,13},{10,... | collective-permute-start | bytes 393224 | tf_op jit(solution)/shard_map/ppermute | solution.py:18
  145.1 24.1 %collective-permute-start.25 = (bf16[2,1024,256]{2,1,0:T(8,128)(2,1)S(1)}, bf16[2,1024,256]{2,1,0:T(8,128)(2,1)S(1)}, u32[]{:S(2)}, u32[]{:S(2)}) collective-permute-start(bf16[2,1024,256]{2,1,0:T(8,128)(2,1)S(1)} %collective-permute-done.24), channel_id=1, source_target_pairs={{0,32},{32,0},{64,96},{96,64},{1,33},{33,1},{65,97},{97,65},{2,34}... | collective-permute-start | bytes 3145736 | tf_op jit(solution)/shard_map/ppermute | solution.py:30
  173.1 28.4 %collective-permute-start.83 = (bf16[64,1024]{1,0:T(8,128)(2,1)S(1)}, bf16[64,1024]{1,0:T(8,128)(2,1)S(1)}, u32[]{:S(2)}, u32[]{:S(2)}) collective-permute-start(bf16[64,1024]{1,0:T(8,128)(2,1)S(1)} %copy-done.34), channel_id=1, source_target_pairs={{0,2},{1,3},{2,4},{3,5},{4,6},{5,7},{6,0},{7,1},{8,10},{9,11},{10,... | collective-permute-start | bytes 393224 | tf_op jit(solution)/shard_map/ppermute | solution.py:18
  174.5 27.1 %collective-permute-start.82 = (bf16[64,1024]{1,0:T(8,128)(2,1)S(1)}, bf16[64,1024]{1,0:T(8,128)(2,1)S(1)}, u32[]{:S(2)}, u32[]{:S(2)}) collective-permute-start(bf16[64,1024]{1,0:T(8,128)(2,1)S(1)} %copy-done.34), channel_id=1, source_target_pairs={{0,4},{1,5},{2,6},{3,7},{4,0},{5,1},{6,2},{7,3},{8,12},{9,13},{10,... | collective-permute-start | bytes 393224 | tf_op jit(solution)/shard_map/ppermute | solution.py:18
  221.9 16.0 %collective-permute-start.111 = (bf16[64,1024]{1,0:T(8,128)(2,1)S(1)}, bf16[64,1024]{1,0:T(8,128)(2,1)S(1)}, u32[]{:S(2)}, u32[]{:S(2)}) collective-permute-start(bf16[64,1024]{1,0:T(8,128)(2,1)S(1)} %get-tuple-element.249), channel_id=1, source_target_pairs={{0,6},{1,7},{2,0},{3,1},{4,2},{5,3},{6,4},{7,5},{8,14},{9,15},{10,... | collective-permute-start | bytes 393224 | tf_op jit(solution)/shard_map/ppermute | solution.py:18
  225.5 15.1 %collective-permute-start.53 = (bf16[64,1024]{1,0:T(8,128)(2,1)S(1)}, bf16[64,1024]{1,0:T(8,128)(2,1)S(1)}, u32[]{:S(2)}, u32[]{:S(2)}) collective-permute-start(bf16[64,1024]{1,0:T(8,128)(2,1)S(1)} %get-tuple-element.266), channel_id=1, source_target_pairs={{0,2},{1,3},{2,4},{3,5},{4,6},{5,7},{6,0},{7,1},{8,10},{9,11},{10,... | collective-permute-start | bytes 393224 | tf_op jit(solution)/shard_map/ppermute | solution.py:18
  248.1 19.1 %collective-permute-start.79 = (bf16[64,1024]{1,0:T(8,128)(2,1)S(1)}, bf16[64,1024]{1,0:T(8,128)(2,1)S(1)}, u32[]{:S(2)}, u32[]{:S(2)}) collective-permute-start(bf16[64,1024]{1,0:T(8,128)(2,1)S(1)} %get-tuple-element.274), channel_id=1, source_target_pairs={{0,4},{1,5},{2,6},{3,7},{4,0},{5,1},{6,2},{7,3},{8,12},{9,13},{10,... | collective-permute-start | bytes 393224 | tf_op jit(solution)/shard_map/ppermute | solution.py:18
  248.3 19.4 %collective-permute-start.28 = (bf16[64,1024]{1,0:T(8,128)(2,1)S(1)}, bf16[64,1024]{1,0:T(8,128)(2,1)S(1)}, u32[]{:S(2)}, u32[]{:S(2)}) collective-permute-start(bf16[64,1024]{1,0:T(8,128)(2,1)S(1)} %get-tuple-element.260), channel_id=1, source_target_pairs={{0,2},{1,3},{2,4},{3,5},{4,6},{5,7},{6,0},{7,1},{8,10},{9,11},{10,... | collective-permute-start | bytes 393224 | tf_op jit(solution)/shard_map/ppermute | solution.py:18
  250.5 19.5 %collective-permute-start.30 = (bf16[64,1024]{1,0:T(8,128)(2,1)S(1)}, bf16[64,1024]{1,0:T(8,128)(2,1)S(1)}, u32[]{:S(2)}, u32[]{:S(2)}) collective-permute-start(bf16[64,1024]{1,0:T(8,128)(2,1)S(1)} %get-tuple-element.261), channel_id=1, source_target_pairs={{0,6},{1,7},{2,0},{3,1},{4,2},{5,3},{6,4},{7,5},{8,14},{9,15},{10,... | collective-permute-start | bytes 393224 | tf_op jit(solution)/shard_map/ppermute | solution.py:18
  253.0 19.1 %collective-permute-start.29 = (bf16[64,1024]{1,0:T(8,128)(2,1)S(1)}, bf16[64,1024]{1,0:T(8,128)(2,1)S(1)}, u32[]{:S(2)}, u32[]{:S(2)}) collective-permute-start(bf16[64,1024]{1,0:T(8,128)(2,1)S(1)} %get-tuple-element.262), channel_id=1, source_target_pairs={{0,4},{1,5},{2,6},{3,7},{4,0},{5,1},{6,2},{7,3},{8,12},{9,13},{10,... | collective-permute-start | bytes 393224 | tf_op jit(solution)/shard_map/ppermute | solution.py:18
  255.5 128.7 %collective-permute-start.180 = (bf16[256,1024]{1,0:T(8,128)(2,1)S(1)}, bf16[256,1024]{1,0:T(8,128)(2,1)S(1)}, u32[]{:S(2)}, u32[]{:S(2)}) collective-permute-start(bf16[256,1024]{1,0:T(8,128)(2,1)S(1)} %slice.1080), channel_id=1, source_target_pairs={{0,32},{32,0},{64,96},{96,64},{1,33},{33,1},{65,97},{97,65},{2,34}... | collective-permute-start | bytes 1572872 | tf_op jit(solution)/shard_map/ppermute | solution.py:30
  291.4 18.1 %collective-permute-start.92 = (bf16[64,256]{1,0:T(8,128)(2,1)S(1)}, bf16[64,256]{1,0:T(8,128)(2,1)S(1)}, u32[]{:S(2)}, u32[]{:S(2)}) collective-permute-start(bf16[64,256]{1,0:T(8,128)(2,1)S(1)} %get-tuple-element.317), channel_id=1, source_target_pairs={{0,24},{8,0},{16,8},{24,16},{1,25},{9,1},{17,9},{25,17},{2,26},{10... | collective-permute-start | bytes 98312 | tf_op jit(solution)/shard_map/ppermute | solution.py:26
  300.9 49.0 %collective-permute-start.119 = (bf16[64,256]{1,0:T(8,128)(2,1)S(1)}, bf16[64,256]{1,0:T(8,128)(2,1)S(1)}, u32[]{:S(2)}, u32[]{:S(2)}) collective-permute-start(bf16[64,256]{1,0:T(8,128)(2,1)S(1)} %get-tuple-element.93), channel_id=1, source_target_pairs={{0,24},{8,0},{16,8},{24,16},{1,25},{9,1},{17,9},{25,17},{2,26},{10... | collective-permute-start | bytes 98312 | tf_op jit(solution)/shard_map/ppermute | solution.py:26
  309.6 48.4 %collective-permute-start.122 = (bf16[64,256]{1,0:T(8,128)(2,1)S(1)}, bf16[64,256]{1,0:T(8,128)(2,1)S(1)}, u32[]{:S(2)}, u32[]{:S(2)}) collective-permute-start(bf16[64,256]{1,0:T(8,128)(2,1)S(1)} %get-tuple-element.96), channel_id=1, source_target_pairs={{0,16},{8,24},{16,0},{24,8},{1,17},{9,25},{17,1},{25,9},{2,18},{10... | collective-permute-start | bytes 98312 | tf_op jit(solution)/shard_map/ppermute | solution.py:26
  321.6 29.8 %collective-permute-start.144 = (bf16[64,256]{1,0:T(8,128)(2,1)S(1)}, bf16[64,256]{1,0:T(8,128)(2,1)S(1)}, u32[]{:S(2)}, u32[]{:S(2)}) collective-permute-start(bf16[64,256]{1,0:T(8,128)(2,1)S(1)} %get-tuple-element.107), channel_id=1, source_target_pairs={{0,24},{8,0},{16,8},{24,16},{1,25},{9,1},{17,9},{25,17},{2,26},{10... | collective-permute-start | bytes 98312 | tf_op jit(solution)/shard_map/ppermute | solution.py:26
  386.7 27.5 %collective-permute-start.154 = (bf16[64,1024]{1,0:T(8,128)(2,1)S(1)}, bf16[64,1024]{1,0:T(8,128)(2,1)S(1)}, u32[]{:S(2)}, u32[]{:S(2)}) collective-permute-start(bf16[64,1024]{1,0:T(8,128)(2,1)S(1)} %get-tuple-element.244), channel_id=1, source_target_pairs={{0,4},{1,5},{2,6},{3,7},{4,0},{5,1},{6,2},{7,3},{8,12},{9,13},{10,... | collective-permute-start | bytes 393224 | tf_op jit(solution)/shard_map/ppermute | solution.py:18
  387.3 27.5 %collective-permute-start.128 = (bf16[64,1024]{1,0:T(8,128)(2,1)S(1)}, bf16[64,1024]{1,0:T(8,128)(2,1)S(1)}, u32[]{:S(2)}, u32[]{:S(2)}) collective-permute-start(bf16[64,1024]{1,0:T(8,128)(2,1)S(1)} %get-tuple-element.245), channel_id=1, source_target_pairs={{0,2},{1,3},{2,4},{3,5},{4,6},{5,7},{6,0},{7,1},{8,10},{9,11},{10,... | collective-permute-start | bytes 393224 | tf_op jit(solution)/shard_map/ppermute | solution.py:18
  387.4 27.4 %collective-permute-start.130 = (bf16[64,1024]{1,0:T(8,128)(2,1)S(1)}, bf16[64,1024]{1,0:T(8,128)(2,1)S(1)}, u32[]{:S(2)}, u32[]{:S(2)}) collective-permute-start(bf16[64,1024]{1,0:T(8,128)(2,1)S(1)} %get-tuple-element.246), channel_id=1, source_target_pairs={{0,6},{1,7},{2,0},{3,1},{4,2},{5,3},{6,4},{7,5},{8,14},{9,15},{10,... | collective-permute-start | bytes 393224 | tf_op jit(solution)/shard_map/ppermute | solution.py:18
  390.0 24.9 %collective-permute-start.129 = (bf16[64,1024]{1,0:T(8,128)(2,1)S(1)}, bf16[64,1024]{1,0:T(8,128)(2,1)S(1)}, u32[]{:S(2)}, u32[]{:S(2)}) collective-permute-start(bf16[64,1024]{1,0:T(8,128)(2,1)S(1)} %get-tuple-element.247), channel_id=1, source_target_pairs={{0,4},{1,5},{2,6},{3,7},{4,0},{5,1},{6,2},{7,3},{8,12},{9,13},{10,... | collective-permute-start | bytes 393224 | tf_op jit(solution)/shard_map/ppermute | solution.py:18
  391.4 53.0 %collective-permute-start.179 = (bf16[256,1024]{1,0:T(8,128)(2,1)S(1)}, bf16[256,1024]{1,0:T(8,128)(2,1)S(1)}, u32[]{:S(2)}, u32[]{:S(2)}) collective-permute-start(bf16[256,1024]{1,0:T(8,128)(2,1)S(1)} %copy-done.32), channel_id=1, source_target_pairs={{0,32},{32,0},{64,96},{96,64},{1,33},{33,1},{65,97},{97,65},{2,34}... | collective-permute-start | bytes 1572872 | tf_op jit(solution)/shard_map/ppermute | solution.py:30
  414.2 30.1 %collective-permute-start.181 = (bf16[256,1024]{1,0:T(8,128)(2,1)S(1)}, bf16[256,1024]{1,0:T(8,128)(2,1)S(1)}, u32[]{:S(2)}, u32[]{:S(2)}) collective-permute-start(bf16[256,1024]{1,0:T(8,128)(2,1)S(1)} %add_convert_fusion.7), channel_id=1, source_target_pairs={{0,65},{1,0},{2,67},{3,2},{4,69},{5,4},{6,71},{7,6},{32,33},{33,96... | collective-permute-start | bytes 1572872 | tf_op jit(solution)/shard_map/ppermute | solution.py:44
  437.3 22.8 %collective-permute-start.168 = (bf16[1024,512]{1,0:T(8,128)(2,1)S(1)}, bf16[1024,512]{1,0:T(8,128)(2,1)S(1)}, u32[]{:S(2)}, u32[]{:S(2)}) collective-permute-start(bf16[1024,512]{1,0:T(8,128)(2,1)S(1)} %pad_maximum_fusion.7), channel_id=1, source_target_pairs={{0,32},{32,0},{64,96},{96,64},{1,33},{33,1},{65,97},{97,65},{2,34}... | collective-permute-start | bytes 3145736 | tf_op jit(solution)/shard_map/ppermute | solution.py:30
  449.8 45.4 %collective-permute-start.167 = (bf16[1024,512]{1,0:T(8,128)(2,1)S(1)}, bf16[1024,512]{1,0:T(8,128)(2,1)S(1)}, u32[]{:S(2)}, u32[]{:S(2)}) collective-permute-start(bf16[1024,512]{1,0:T(8,128)(2,1)S(1)} %pad_maximum_fusion.6), channel_id=1, source_target_pairs={{0,32},{32,0},{64,96},{96,64},{1,33},{33,1},{65,97},{97,65},{2,34}... | collective-permute-start | bytes 3145736 | tf_op jit(solution)/shard_map/ppermute | solution.py:30
  451.9 19.0 %collective-permute-start.156 = (bf16[256,1024]{1,0:T(8,128)(2,1)S(1)}, bf16[256,1024]{1,0:T(8,128)(2,1)S(1)}, u32[]{:S(2)}, u32[]{:S(2)}) collective-permute-start(bf16[256,1024]{1,0:T(8,128)(2,1)S(1)} %get-tuple-element.206), channel_id=1, source_target_pairs={{0,32},{32,0},{64,96},{96,64},{1,33},{33,1},{65,97},{97,65},{2,34}... | collective-permute-start | bytes 1572872 | tf_op jit(solution)/shard_map/ppermute | solution.py:30
  470.0 25.2 %collective-permute-start.169 = (bf16[1024,512]{1,0:T(8,128)(2,1)S(1)}, bf16[1024,512]{1,0:T(8,128)(2,1)S(1)}, u32[]{:S(2)}, u32[]{:S(2)}) collective-permute-start(bf16[1024,512]{1,0:T(8,128)(2,1)S(1)} %add_convert_fusion.4), channel_id=1, source_target_pairs={{0,65},{1,0},{2,67},{3,2},{4,69},{5,4},{6,71},{7,6},{32,33},{33,96... | collective-permute-start | bytes 3145736 | tf_op jit(solution)/shard_map/ppermute | solution.py:44
  489.4 29.1 %collective-permute-start.189 = (bf16[256,1024]{1,0:T(8,128)(2,1)S(1)}, bf16[256,1024]{1,0:T(8,128)(2,1)S(1)}, u32[]{:S(2)}, u32[]{:S(2)}) collective-permute-start(bf16[256,1024]{1,0:T(8,128)(2,1)S(1)} %constant_dynamic-slice_fusion), channel_id=1, source_target_pairs={{0,32},{32,0},{64,96},{96,64},{1,33},{33,1},{65,97},{97,65},{2,34}... | collective-permute-start | bytes 1572872 | tf_op jit(solution)/shard_map/ppermute | solution.py:30
  512.4 23.6 %collective-permute-start.166 = (bf16[1,256,1024]{2,1,0:T(8,128)(2,1)S(1)}, bf16[1,256,1024]{2,1,0:T(8,128)(2,1)S(1)}, u32[]{:S(2)}, u32[]{:S(2)}) collective-permute-start(bf16[1,256,1024]{2,1,0:T(8,128)(2,1)S(1)} %dynamic-slice_bitcast_fusion), channel_id=1, source_target_pairs={{0,32},{32,0},{64,96},{96,64},{1,33},{33,1},{65,97},{97,65},{2,34}... | collective-permute-start | bytes 1572872 | tf_op jit(solution)/shard_map/ppermute | solution.py:30
  (236 other events, 1815.8 us)
